TPU v7x, 1024 devices: a whole 8x8x8 slice. The times are simulated.
1024 devices in a mesh: context: 64 (over x, z), dp: 2 (over y_hi), tensor: 8 (over y_lo, core).
Axes of the slice: x: 8, y: 8 (y_hi: 2, y_lo: 4; y = y_hi * 4 + y_lo), z: 8, core: 2. Of those that a mesh axis runs over, the one named last changes fastest.
Arguments:
- queries: bfloat16 [2, 16384, 8192], P('dp', 'context', 'tensor'), may hold values from -6 to 6
- keys_values: bfloat16 [2, 16384, 2048], P('dp', 'context', 'tensor'), may hold values from -6 to 6
- outputs: bfloat16 [2, 16384, 8192], P('dp', 'context', 'tensor'), may hold values from -3 to 3
- grad_out: bfloat16 [2, 16384, 8192], P('dp', 'context', 'tensor'), may hold values from -48 to 48
- logsumexp: float32 [2, 64, 16384], P('dp', 'tensor', 'context'), may hold values from 4.5 to 6.5
- doc_ids: int32 [2, 16384], P('dp'), may hold values from 0 to 3, as said below
- inputs: bfloat16 [2, 16384, 4096], P('dp', 'context'), may hold values from -0.1875 to 0.1875
Outputs:
- grad_queries: bfloat16 [2, 16384, 8192], P('dp', 'context', 'tensor')
- grad_keys_values: bfloat16 [2, 16384, 2048], P('dp', 'context', 'tensor')
- grad_value_proj: float32 [8, 4096, 128], P('tensor', ('context', 'dp'))
Inputs may be any that keep to these rules, and one draw needn't show every extreme that they name: `doc_ids`: for each sequence, the ids never fall along token position pos, each of the 4 documents holds one or more tokens, and the last document holds every token from position (63) * (128) on.
All inputs are finite; a program needn't handle non-finite values.
Results may differ from a plain program's by a relative error of at most 0.0049.
Values may be sent and summed in bfloat16 or wider, within the bound.
No kernel may reach another device: no remote copies, remote signals or barrier semaphores. Data moves between devices by JAX's collectives and lax.ppermute only.
A program may use at most 32 MiB of HBM per device.

v0:
```python
import jax
import jax.numpy as jnp
from jax import lax
from jax.sharding import PartitionSpec as P

HD = 128


def shifted(block, axis, distance):
    devices = range(lax.axis_size(axis))
    route = [((i - distance) % len(devices), i) for i in devices]
    return lax.ppermute(block, axis, route)


def token_positions(device, tok_rows, cycle_size):
    half_len = tok_rows // 2
    offsets = jnp.arange(tok_rows, dtype=jnp.int32)
    early = offsets < half_len
    later = (2 * cycle_size - 1 - device) * half_len + offsets - half_len
    return jnp.where(early, device * half_len + offsets, later)


def per_device(queries, keys_values, outputs, grad_out, logsumexp, doc_ids, inputs):
    tok_rows = queries.shape[1]
    head_dim = HD
    group_size = queries.shape[2] // head_dim
    cycle_size = lax.axis_size("context")
    cycle_index = lax.axis_index("context")
    prev_index = (cycle_index - 1 + cycle_size) % cycle_size
    scaling = head_dim ** (-0.5)
    visiting = shifted(keys_values, "context", 1)
    key_value_rows = jnp.concatenate([keys_values[0], visiting[0]], axis=0)
    key_rows = key_value_rows[:, :head_dim]
    value_rows = key_value_rows[:, head_dim:]
    seq_docs = doc_ids[0]
    own_docs = lax.dynamic_slice_in_dim(seq_docs, cycle_index * tok_rows, tok_rows)
    prev_docs = lax.dynamic_slice_in_dim(seq_docs, prev_index * tok_rows, tok_rows)
    query_pos = token_positions(cycle_index, tok_rows, cycle_size)
    key_pos = jnp.concatenate([query_pos, token_positions(prev_index, tok_rows, cycle_size)])
    key_docs = jnp.concatenate([own_docs, prev_docs])
    visible = (key_pos[None, :] <= query_pos[:, None]) & (key_docs[None, :] == own_docs[:, None])
    query_block = queries[0].reshape(tok_rows, group_size, head_dim)
    grad_block = grad_out[0].reshape(tok_rows, group_size, head_dim)
    output_block = outputs[0].reshape(tok_rows, group_size, head_dim)
    lse_block = logsumexp[0]
    scores = jnp.einsum("qgd,kd->gqk", query_block, key_rows, preferred_element_type=jnp.float32)
    attn_prob = jnp.where(
        visible[None], jnp.exp(scores * scaling - lse_block[:, :, None]), jnp.float32(0.0)
    )
    row_delta = jnp.sum(grad_block.astype(jnp.float32) * output_block.astype(jnp.float32), axis=2).T
    grad_prob = jnp.einsum(
        "qgd,kd->gqk", grad_block, value_rows, preferred_element_type=jnp.float32
    )
    grad_score = attn_prob * (grad_prob - row_delta[:, :, None])
    prob_half = attn_prob.astype(jnp.bfloat16)
    score_half = grad_score.astype(jnp.bfloat16)
    value_grad = jnp.einsum(
        "gqk,qgd->kd", prob_half, grad_block, preferred_element_type=jnp.float32
    )
    key_grad = scaling * jnp.einsum(
        "gqk,qgd->kd", score_half, query_block, preferred_element_type=jnp.float32
    )
    query_grad = scaling * jnp.einsum(
        "gqk,kd->qgd", score_half, key_rows, preferred_element_type=jnp.float32
    )
    local_grad = jnp.concatenate([key_grad, value_grad], axis=1)
    returned = shifted(local_grad[tok_rows:], "context", -1)
    grad_kv = (local_grad[:tok_rows] + returned).astype(jnp.bfloat16)
    value_half = grad_kv[:, head_dim:]
    features = inputs[0]
    dp_size = lax.axis_size("dp")
    share_rows = features.shape[1] // (cycle_size * dp_size)
    proj_grad = lax.psum_scatter(
        lax.dot_general(
            features, value_half, (((0,), (0,)), ((), ())), preferred_element_type=jnp.float32
        ),
        ("context", "dp"),
        scatter_dimension=0,
        tiled=True,
    )
    grad_queries = query_grad.astype(jnp.bfloat16).reshape(1, tok_rows, group_size * head_dim)
    return (
        grad_queries,
        grad_kv.reshape(1, tok_rows, 2 * head_dim),
        proj_grad.reshape(1, share_rows, head_dim),
    )


def solution(mesh):
    in_specs = (
        P("dp", "context", "tensor"),
        P("dp", "context", "tensor"),
        P("dp", "context", "tensor"),
        P("dp", "context", "tensor"),
        P("dp", "tensor", "context"),
        P("dp", None),
        P("dp", "context", None),
    )
    out_specs = (
        P("dp", "context", "tensor"),
        P("dp", "context", "tensor"),
        P("tensor", ("context", "dp"), None),
    )
    return jax.shard_map(
        per_device, mesh=mesh, in_specs=in_specs, out_specs=out_specs, check_vma=False
    )
```

profile of v0, /device:TPU:16, one launch (start us, length us, event | category | flops | bytes accessed | tf_op | source)
XLA Modules:
  0.0 937.2 jit_solution(6133679131833802338)
XLA Ops:
  7.2 0.0 copy-start
  7.2 0.0 reduce-scatter.4.cloned.1.call-start
  7.2 5.3 collective-permute-start
  12.6 0.0 copy-start.2
  12.6 1.3 copy.40
  13.9 1.1 copy.41
  15.0 1.1 copy.29
  16.1 1.1 convert_bitcast_fusion
  17.3 0.0 copy-start.4
  17.3 0.2 copy.42
  17.5 0.3 multiply_reduce_fusion
  17.9 0.1 copy.23
  17.9 0.7 constant_dynamic-slice_fusion
  18.7 0.2 compare_and_fusion
  18.9 11.8 %collective-permute-done = bf16[1,256,256]{2,1,0:T(8,128)(2,1)S(1)} collective-permute-done((bf16[1,256,256]{2,1,0:T(8,128)(2,1)}, bf16[1,256,256]{2,1,0:T(8,128)(2,1)S(1)}, u32[]{:S(2)}, u32[]{:S(2)}) %collective-permute-start) | collective-permute-done | bytes 131104 | tf_op jit(solution)/shard_map/ppermute | solution.py:12
  30.7 0.0 copy-done.2
  30.7 0.7 fusion.23
  31.4 0.0 copy-start.3
  31.4 0.0 copy-done.4
  31.4 2.1 fusion.10
  33.5 0.0 copy-done.3
  33.5 1.4 fusion.1
  34.9 0.0 copy-start.1
  34.9 1.3 copy-done.1
  36.3 0.8 fusion.13
  37.1 4.6 collective-permute-start.1
  41.7 5.5 collective-permute-done.1
  47.3 0.0 copy-done
  47.3 1.8 convolution_bitcast_fusion
  49.1 2.9 copy.38
  52.0 0.0 reduce-scatter.4.cloned.1.call-update
  52.0 2.1 fusion.9
  54.0 1.0 copy.30
  55.1 0.8 copy.31
  55.8 873.0 %reduce-scatter.4.cloned.1.call-done = f32[32,128]{1,0:T(8,128)} async-done(((f32[4096,128]{1,0:T(8,128)}), f32[32,128]{1,0:T(8,128)}) %reduce-scatter.4.cloned.1.call-update) | async-done | bytes 16400
  928.8 0.8 copy.39
  929.7 0.7 copy.32
  (5 shorter events, 0.1 us)
Async XLA Ops:
  7.2 40.1 %copy-start = (bf16[1,256,4096]{2,1,0:T(8,128)(2,1)S(1)}, bf16[1,256,4096]{2,1,0:T(8,128)(2,1)}, u32[]{:S(2)}) copy-start(bf16[1,256,4096]{2,1,0:T(8,128)(2,1)} %param.13) | copy-start | bytes 6291460
  7.2 921.7 %reduce-scatter.4.cloned.1.call-start = ((), (), s32[]{:S(2)}) async-start(), calls=%async_computation.1 | async-start | bytes 2113536
  7.2 23.5 %collective-permute-start = (bf16[1,256,256]{2,1,0:T(8,128)(2,1)}, bf16[1,256,256]{2,1,0:T(8,128)(2,1)S(1)}, u32[]{:S(2)}, u32[]{:S(2)}) collective-permute-start(bf16[1,256,256]{2,1,0:T(8,128)(2,1)} %param.8), channel_id=1, source_target_pairs={{1008,0},{0,16},{16,32},{32,48},{48,64},{64,80},{80,96},{96,112},{... | collective-permute-start | bytes 393224 | tf_op jit(solution)/shard_map/ppermute | solution.py:12
  12.6 18.1 %copy-start.2 = (bf16[1,256,256]{2,1,0:T(8,128)(2,1)S(1)}, bf16[1,256,256]{2,1,0:T(8,128)(2,1)}, u32[]{:S(2)}) copy-start(bf16[1,256,256]{2,1,0:T(8,128)(2,1)} %param.8) | copy-start | bytes 393220
  17.3 14.1 %copy-start.4 = (f32[1,8,256]{2,1,0:T(8,128)S(1)}, f32[1,8,256]{2,1,0:T(8,128)}, u32[]{:S(2)}) copy-start(f32[1,8,256]{2,1,0:T(8,128)} %param.11) | copy-start | bytes 24580
  31.4 2.1 copy-start.3
  34.9 1.4 copy-start.1
  37.1 10.1 %collective-permute-start.1 = (f32[256,256]{0,1:T(8,128)S(1)}, f32[256,256]{0,1:T(8,128)S(1)}, u32[]{:S(2)}, u32[]{:S(2)}) collective-permute-start(f32[256,256]{0,1:T(8,128)S(1)} %pad_maximum_fusion), channel_id=1, source_target_pairs={{16,0},{32,16},{48,32},{64,48},{80,64},{96,80},{112,96},{128,112},... | collective-permute-start | bytes 786440 | tf_op jit(solution)/shard_map/ppermute | solution.py:12
Sparse Core Ops, SparseCore 0:
  52.1 876.6 reduce-scatter.3
where the time goes:
time: 938 us; the launch traced here: 937 us
  waiting for transfers between devices  890 us (95%)
  between operations  14.2 us (2%)
  local copies, waits for them, and re-layouts  12 us (1%)
  starting transfers between devices  9.93 us (1%)
    unnamed x2, waiting for transfers between devices  873 us
  transfers between devices with their start and end apart: 3, of which 3 were waited for; matrix products, arithmetic and copies ran while one was open for 1% of the time, Pallas kernels for 0%

commit v1 on v0

--- a/solution.py
+++ b/solution.py
@@ -70,13 +70,12 @@
     features = inputs[0]
     dp_size = lax.axis_size("dp")
     share_rows = features.shape[1] // (cycle_size * dp_size)
-    proj_grad = lax.psum_scatter(
-        lax.dot_general(
-            features, value_half, (((0,), (0,)), ((), ())), preferred_element_type=jnp.float32
-        ),
-        ("context", "dp"),
-        scatter_dimension=0,
-        tiled=True,
+    partial = lax.dot_general(
+        features, value_half, (((0,), (0,)), ((), ())), preferred_element_type=jnp.float32
+    ).astype(jnp.bfloat16)
+    shares = lax.all_to_all(partial, ("context", "dp"), 0, 0, tiled=True)
+    proj_grad = jnp.sum(
+        shares.reshape(cycle_size * dp_size, share_rows, head_dim).astype(jnp.float32), axis=0
     )
     grad_queries = query_grad.astype(jnp.bfloat16).reshape(1, tok_rows, group_size * head_dim)
     return (

time: 938 us -> 93.3 us (0.10)
  the two profiles are of different devices: /device:TPU:16 before, /device:TPU:2 now
where the time goes in v1:
time: 93.3 us; the launch traced here: 92.8 us
  waiting for transfers between devices  42.8 us (46%)
  starting transfers between devices  28.3 us (30%)
  local copies, waits for them, and re-layouts  9.98 us (11%)
  matrix products  8.3 us (9%)
  other arithmetic  2.59 us (3%)
    all_to_all x1, waiting for transfers between devices, per_device(): shares = lax.all_to_all(partial, ('context', 'dp'), 0, 0, tiled=True)  27.8 us
    all_to_all x1, starting transfers between devices, per_device(): shares = lax.all_to_all(partial, ('context', 'dp'), 0, 0, tiled=True)  18.4 us
    ppermute x2, waiting for transfers between devices, shifted(): return lax.ppermute(block, axis, route)  15 us
    ppermute x2, starting transfers between devices, shifted(): return lax.ppermute(block, axis, route)  9.89 us
    unnamed x14, local copies, waits for them, and re-layouts  5.49 us
    dot_general x1, matrix products, per_device(): jnp.einsum('gqk,kd->qgd', score_half, key_rows, preferred_element_type=jn...  2.86 us
    dot_general x1, matrix products, per_device(): jnp.einsum('gqk,qgd->kd', prob_half, grad_block, preferred_element_type=j...  2.12 us
  transfers between devices with their start and end apart: 3, of which 3 were waited for; matrix products, arithmetic and copies ran while one was open for 13% of the time, Pallas kernels for 0%

profile of v1, /device:TPU:2, one launch (start us, length us, event | category | flops | bytes accessed | tf_op | source)
XLA Modules:
  0.0 92.8 jit_solution(2527199596396434266)
XLA Ops:
  0.6 0.0 copy-start
  0.6 5.3 %collective-permute-start = (bf16[1,256,256]{2,1,0:T(8,128)(2,1)}, bf16[1,256,256]{2,1,0:T(8,128)(2,1)S(1)}, u32[]{:S(2)}, u32[]{:S(2)}) collective-permute-start(bf16[1,256,256]{2,1,0:T(8,128)(2,1)} %param.8), channel_id=1, source_target_pairs={{1008,0},{0,16},{16,32},{32,48},{48,64},{64,80},{80,96},{96,112},{... | collective-permute-start | bytes 393224 | tf_op jit(solution)/shard_map/ppermute | solution.py:12
  6.0 0.0 copy-start.2
  6.0 1.3 %copy.48 = bf16[1,256,1024]{1,2,0:T(8,128)(2,1)S(1)} copy(bf16[1,256,1024]{2,1,0:T(8,128)(2,1)} %param.7) | data formatting | bytes 1048576 | tf_op jit(solution)/shard_map/reshape;squeeze | solution.py:42
  7.3 1.1 %copy.49 = bf16[32,8,8,128]{3,2,1,0:T(8,128)(2,1)S(1)} copy(bf16[32,8,8,128]{3,1,2,0:T(8,128)(2,1)} %bitcast.78) | data formatting | bytes 1048576
  8.4 1.1 %copy.39 = bf16[256,8,128]{0,2,1:T(8,128)(2,1)} copy(bf16[256,8,128]{2,1,0:T(8,128)(2,1)S(1)} %bitcast.66) | data formatting | bytes 1048576 | tf_op jit(solution)/shard_map/reshape;squeeze | solution.py:43
  9.6 1.1 %convert_bitcast_fusion = f32[32,8,8,128]{3,1,2,0:T(8,128)S(1)} fusion(bf16[1,256,1024]{2,1,0:T(8,128)(2,1)} %param.9), kind=kLoop, calls=%fused_computation.18 | loop fusion | flops 262144 | bytes 1572864
  10.7 0.0 copy-start.4
  10.7 0.2 copy.50
  10.9 0.3 multiply_reduce_fusion
  11.3 0.1 copy.33
  11.4 0.7 constant_dynamic-slice_fusion
  12.1 0.2 compare_and_fusion
  12.3 9.5 %collective-permute-done = bf16[1,256,256]{2,1,0:T(8,128)(2,1)S(1)} collective-permute-done((bf16[1,256,256]{2,1,0:T(8,128)(2,1)}, bf16[1,256,256]{2,1,0:T(8,128)(2,1)S(1)}, u32[]{:S(2)}, u32[]{:S(2)}) %collective-permute-start) | collective-permute-done | bytes 131104 | tf_op jit(solution)/shard_map/ppermute | solution.py:12
  21.8 0.0 copy-done.2
  21.8 0.7 fusion.24
  22.5 0.0 copy-start.3
  22.5 0.0 copy-done.4
  22.5 2.1 %fusion.11 = f32[512,128]{0,1:T(8,128)S(1)} fusion(bf16[256,8,128]{0,2,1:T(8,128)(2,1)} %copy.39, f32[512,256,8]{1,0,2:T(8,128)S(1)} %fusion.24, f32[8,256]{1,0:T(8,128)S(1)} %bitcast.84, pred[256,512]{0,1:T(8,128)(4,1)S(1)} %compare_and_fusion), kind=kOutput, calls=%fused_computation.15 | convolution fusion | flops 272629760 | bytes 5120000 | tf_op jit(solution)/shard_map/gqk,qgd->kd/dot_general | solution.py:57
  24.6 0.0 copy-done.3
  24.6 1.4 %fusion.2 = bf16[8,256,512]{1,2,0:T(8,128)(2,1)S(1)} fusion(f32[512,256,8]{1,0,2:T(8,128)S(1)} %fusion.24, bf16[256,8,128]{0,2,1:T(8,128)(2,1)S(1)} %copy-done.3, f32[8,256]{1,0:T(8,128)S(1)} %copy.33, f32[8,256]{1,0:T(8,128)S(1)} %bitcast.85, pred[256,512]{0,1:T(8,128)(4,1)S(1)} %compare_and_fusion, bf16[256,256]{1,0:T(8,128)(2,1)S(1)} %bitcast.76, ...), kind=kOutput, calls=%fused_computation.4 | convolution fusion | flops 274989056 | bytes 7225344 | tf_op jit(solution)/shard_map/qgd,kd->gqk/dot_general | solution.py:51
  26.0 0.0 copy-start.1
  26.0 1.3 %copy-done.1 = bf16[8,256,512]{1,2,0:T(8,128)(2,1)} copy-done((bf16[8,256,512]{1,2,0:T(8,128)(2,1)}, bf16[8,256,512]{1,2,0:T(8,128)(2,1)S(1)}, u32[]{:S(2)}) %copy-start.1) | copy-done | bytes 2097176
  27.3 0.8 fusion.14
  28.2 4.6 %collective-permute-start.1 = (f32[256,256]{0,1:T(8,128)S(1)}, f32[256,256]{0,1:T(8,128)S(1)}, u32[]{:S(2)}, u32[]{:S(2)}) collective-permute-start(f32[256,256]{0,1:T(8,128)S(1)} %pad_maximum_fusion), channel_id=1, source_target_pairs={{16,0},{32,16},{48,32},{64,48},{80,64},{96,80},{112,96},{128,112},... | collective-permute-start | bytes 786440 | tf_op jit(solution)/shard_map/ppermute | solution.py:12
  32.8 5.5 %collective-permute-done.1 = f32[256,256]{0,1:T(8,128)S(1)} collective-permute-done((f32[256,256]{0,1:T(8,128)S(1)}, f32[256,256]{0,1:T(8,128)S(1)}, u32[]{:S(2)}, u32[]{:S(2)}) %collective-permute-start.1) | collective-permute-done | bytes 262176 | tf_op jit(solution)/shard_map/ppermute | solution.py:12
  38.3 0.0 copy-done
  38.4 0.4 fusion
  38.8 1.3 %copy.40 = bf16[4096,128]{1,0:T(8,128)(2,1)} copy(bf16[4096,128]{0,1:T(8,128)(2,1)S(1)} %fusion) | data formatting | bytes 2097152 | tf_op jit(solution)/shard_map/convert_element_type | solution.py:75
  40.1 18.4 %all-to-all-start = ((bf16[128,32,128]{2,1,0:T(8,128)(2,1)}), bf16[128,32,128]{2,1,0:T(8,128)(2,1)S(1)}, u32[]{:S(2)}, u32[]{:S(2)}) async-start(bf16[128,32,128]{2,1,0:T(8,128)(2,1)} %bitcast.68), calls=%async_computation | async-start | bytes 2097152 | tf_op jit(solution)/shard_map/all_to_all | solution.py:76
  58.5 2.9 %fusion.10 = bf16[128,8,256]{2,0,1:T(8,128)(2,1)} fusion(bf16[8,256,512]{1,2,0:T(8,128)(2,1)} %copy-done.1, bf16[256,256]{1,0:T(8,128)(2,1)S(1)} %bitcast.74, bf16[256,256]{1,0:T(8,128)(2,1)S(1)} %bitcast.77), kind=kOutput, calls=%fused_computation.14 | convolution fusion | flops 269221888 | bytes 2883584 | tf_op jit(solution)/shard_map/gqk,kd->qgd/dot_general | solution.py:63
  61.4 2.0 %copy.41 = bf16[1,256,1024]{2,1,0:T(8,128)(2,1)} copy(bf16[1,256,1024]{1,2,0:T(8,128)(2,1)} %bitcast.70) | data formatting | bytes 1048576
  63.4 0.8 copy.42
  64.2 27.8 %all-to-all-done = bf16[128,32,128]{2,1,0:T(8,128)(2,1)S(1)} async-done(((bf16[128,32,128]{2,1,0:T(8,128)(2,1)}), bf16[128,32,128]{2,1,0:T(8,128)(2,1)S(1)}, u32[]{:S(2)}, u32[]{:S(2)}) %all-to-all-start) | async-done | bytes 1048608 | tf_op jit(solution)/shard_map/all_to_all | solution.py:76
  92.0 0.8 convert_reduce_fusion
  (5 shorter events, 0.1 us)
Async XLA Ops:
  0.6 37.7 %copy-start = (bf16[1,256,4096]{2,1,0:T(8,128)(2,1)S(1)}, bf16[1,256,4096]{2,1,0:T(8,128)(2,1)}, u32[]{:S(2)}) copy-start(bf16[1,256,4096]{2,1,0:T(8,128)(2,1)} %param.13) | copy-start | bytes 6291460
  0.6 21.1 %collective-permute-start = (bf16[1,256,256]{2,1,0:T(8,128)(2,1)}, bf16[1,256,256]{2,1,0:T(8,128)(2,1)S(1)}, u32[]{:S(2)}, u32[]{:S(2)}) collective-permute-start(bf16[1,256,256]{2,1,0:T(8,128)(2,1)} %param.8), channel_id=1, source_target_pairs={{1008,0},{0,16},{16,32},{32,48},{48,64},{64,80},{80,96},{96,112},{... | collective-permute-start | bytes 393224 | tf_op jit(solution)/shard_map/ppermute | solution.py:12
  6.0 15.8 %copy-start.2 = (bf16[1,256,256]{2,1,0:T(8,128)(2,1)S(1)}, bf16[1,256,256]{2,1,0:T(8,128)(2,1)}, u32[]{:S(2)}) copy-start(bf16[1,256,256]{2,1,0:T(8,128)(2,1)} %param.8) | copy-start | bytes 393220
  10.7 11.8 %copy-start.4 = (f32[1,8,256]{2,1,0:T(8,128)S(1)}, f32[1,8,256]{2,1,0:T(8,128)}, u32[]{:S(2)}) copy-start(f32[1,8,256]{2,1,0:T(8,128)} %param.11) | copy-start | bytes 24580
  22.5 2.1 %copy-start.3 = (bf16[256,8,128]{0,2,1:T(8,128)(2,1)S(1)}, bf16[256,8,128]{0,2,1:T(8,128)(2,1)}, u32[]{:S(2)}) copy-start(bf16[256,8,128]{0,2,1:T(8,128)(2,1)} %copy.39) | copy-start | bytes 1572868
  26.0 1.3 %copy-start.1 = (bf16[8,256,512]{1,2,0:T(8,128)(2,1)}, bf16[8,256,512]{1,2,0:T(8,128)(2,1)S(1)}, u32[]{:S(2)}) copy-start(bf16[8,256,512]{1,2,0:T(8,128)(2,1)S(1)} %fusion.2) | copy-start | bytes 6291460
  28.2 10.1 %collective-permute-start.1 = (f32[256,256]{0,1:T(8,128)S(1)}, f32[256,256]{0,1:T(8,128)S(1)}, u32[]{:S(2)}, u32[]{:S(2)}) collective-permute-start(f32[256,256]{0,1:T(8,128)S(1)} %pad_maximum_fusion), channel_id=1, source_target_pairs={{16,0},{32,16},{48,32},{64,48},{80,64},{96,80},{112,96},{128,112},... | collective-permute-start | bytes 786440 | tf_op jit(solution)/shard_map/ppermute | solution.py:12
  40.1 51.9 %all-to-all-start = ((bf16[128,32,128]{2,1,0:T(8,128)(2,1)}), bf16[128,32,128]{2,1,0:T(8,128)(2,1)S(1)}, u32[]{:S(2)}, u32[]{:S(2)}) async-start(bf16[128,32,128]{2,1,0:T(8,128)(2,1)} %bitcast.68), calls=%async_computation | async-start | bytes 2097152 | tf_op jit(solution)/shard_map/all_to_all | solution.py:76

commit v2 on v1

v2 whole, which is shorter than its diff:
```python
import functools
import math

import jax
import jax.numpy as jnp
from jax import lax
from jax.experimental import pallas as pl
from jax.experimental.pallas import tpu as pltpu
from jax.sharding import PartitionSpec as P

HD = 128
HALF = 128
F32 = jnp.float32
BF16 = jnp.bfloat16
LOG2E = 1.0 / math.log(2.0)
SCALING = HD ** -0.5
NT = (((1,), (1,)), ((), ()))
NN = (((1,), (0,)), ((), ()))
TN = (((0,), (0,)), ((), ()))


def dot(a, b, dims):
    return lax.dot_general(a, b, dims, preferred_element_type=F32)


def shifted(block, axis, distance):
    devices = range(lax.axis_size(axis))
    route = [((i - distance) % len(devices), i) for i in devices]
    return lax.ppermute(block, axis, route)


def down(row):
    return jnp.transpose(jnp.broadcast_to(row, (HALF, HALF)))


def halves(docs_ref, stretch):
    row = docs_ref[stretch].astype(F32)
    return row[:, :HALF], row[:, HALF:]


def own_masks(docs_ref):
    early, late = halves(docs_ref, 0)
    early_down, late_down = down(early), down(late)
    causal = lax.broadcasted_iota(jnp.int32, (HALF, HALF), 0) <= lax.broadcasted_iota(
        jnp.int32, (HALF, HALF), 1
    )
    return causal & (early_down == early), early_down == late, causal & (late_down == late)


def prev_masks(docs_ref, is_first):
    early, late = halves(docs_ref, 0)
    key_early, key_late = halves(docs_ref, 1)
    key_other = jnp.where(is_first, key_late, key_early)
    return down(key_early) == late, down(key_other) == jnp.where(is_first, late, early)


def other_offset():
    return pl.multiple_of(jnp.where(lax.axis_index("context") == 0, HALF, 0), HALF)


def prob_of(scores, lse_row, visible):
    return jnp.where(
        visible, jnp.exp2(scores * (SCALING * LOG2E) - lse_row * LOG2E), jnp.float32(0.0)
    )


def swap_order(x_size, z_size):
    odd = lax.rem(lax.axis_index("tensor"), 2)
    return lambda x, z: jnp.where(odd == 1, x * z_size + z, z * x_size + x)


def own_values(
    heads, cycle_size, x_size, z_size, q_hbm, kv_hbm, lse_hbm, do_hbm, docs_hbm, x_hbm,
    dv_ref, xt_ref, q_ref, kv_ref, lse_ref, do_ref, docs_ref, x_ref, sems,
):
    me = lax.axis_index("context")
    prev = lax.rem(me + cycle_size - 1, cycle_size)
    rows = 2 * HALF

    def docs_of(stretch):
        return docs_hbm.at[:, pl.ds(pl.multiple_of(stretch * rows, rows), rows)]

    pairs = [
        (q_hbm, q_ref), (kv_hbm, kv_ref), (lse_hbm, lse_ref), (do_hbm, do_ref),
        (docs_of(me), docs_ref.at[0]), (docs_of(prev), docs_ref.at[1]), (x_hbm, x_ref),
    ]
    copies = [
        pltpu.make_async_copy(source, target, sems.at[i])
        for i, (source, target) in enumerate(pairs)
    ]
    for copy in copies:
        copy.start()
    for copy in copies[:-1]:
        copy.wait()
    see_ee, see_el, see_ll = own_masks(docs_ref)
    key_early, key_late = kv_ref[0, :HALF, :HD], kv_ref[0, HALF:, :HD]
    early = jnp.zeros((HALF, HD), F32)
    late = jnp.zeros((HALF, HD), F32)
    for h in range(heads):
        cols = slice(h * HD, (h + 1) * HD)
        scores_early = dot(key_early, q_ref[0, :, cols], NT)
        scores_late = dot(key_late, q_ref[0, HALF:, cols], NT)
        lse_e, lse_l = lse_ref[0, h : h + 1, :HALF], lse_ref[0, h : h + 1, HALF:]
        prob_early = jnp.concatenate(
            [
                prob_of(scores_early[:, :HALF], lse_e, see_ee).astype(BF16),
                prob_of(scores_early[:, HALF:], lse_l, see_el).astype(BF16),
            ],
            axis=1,
        )
        prob_late = prob_of(scores_late, lse_l, see_ll).astype(BF16)
        early = early + dot(prob_early, do_ref[0, :, cols], NN)
        late = late + dot(prob_late, do_ref[0, HALF:, cols], NN)
    dv_ref[:HALF] = early
    dv_ref[HALF:] = late
    copies[-1].wait()
    place = swap_order(x_size, z_size)
    chunk = x_ref.shape[2] // (x_size * z_size)
    for x in range(x_size):
        wide = chunk * z_size
        turned = jnp.transpose(x_ref[0, :, x * wide : (x + 1) * wide])
        for z in range(z_size):
            start = pl.multiple_of(place(x, z) * chunk, chunk)
            xt_ref[pl.ds(start, chunk)] = turned[z * chunk : (z + 1) * chunk]


def prev_values(heads, q_ref, kv_ref, lse_ref, do_ref, docs_ref, dv_ref):
    offset = other_offset()
    see_late, see_other = prev_masks(docs_ref, offset > 0)
    key_early, key_other = kv_ref[0, :HALF, :HD], kv_ref[0, pl.ds(offset, HALF), :HD]
    first = jnp.zeros((HALF, HD), F32)
    other = jnp.zeros((HALF, HD), F32)
    for h in range(heads):
        cols = slice(h * HD, (h + 1) * HD)
        scores_late = dot(key_early, q_ref[0, HALF:, cols], NT)
        scores_other = dot(key_other, q_ref[0, pl.ds(offset, HALF), cols], NT)
        lse_l = lse_ref[0, h : h + 1, HALF:]
        lse_o = lse_ref[0, h : h + 1, pl.ds(offset, HALF)]
        prob_late = prob_of(scores_late, lse_l, see_late).astype(BF16)
        prob_other = prob_of(scores_other, lse_o, see_other).astype(BF16)
        first = first + dot(prob_late, do_ref[0, HALF:, cols], NN)
        other = other + dot(prob_other, do_ref[0, pl.ds(offset, HALF), cols], NN)
    is_first = offset > 0
    dv_ref[:HALF] = jnp.where(is_first, first, first + other).astype(BF16)
    dv_ref[HALF:] = jnp.where(is_first, other, jnp.zeros_like(other)).astype(BF16)


def project(xt_ref, own_ref, back_ref, part_hbm, dv_ref, part_ref, sems):
    value_half = (own_ref[...] + back_ref[...].astype(F32)).astype(BF16)
    dv_ref[...] = value_half
    pieces = sems.shape[0]
    rows = part_ref.shape[0] // pieces
    copies = []
    for i in range(pieces):
        piece = slice(i * rows, (i + 1) * rows)
        part_ref[piece] = dot(xt_ref[piece], value_half, NN).astype(BF16)
        copies.append(
            pltpu.make_async_copy(part_ref.at[piece], part_hbm.at[piece], sems.at[i])
        )
        copies[-1].start()
    for copy in copies:
        copy.wait()


def rest(
    heads, q_ref, kv_ref, prev_ref, lse_ref, do_ref, out_ref, docs_ref, after_ref,
    dq_ref, dk_ref, dk_prev_ref, acc_ref,
):
    offset = other_offset()
    see_ee, see_el, see_ll = own_masks(docs_ref)
    see_pl, see_other = prev_masks(docs_ref, offset > 0)
    key_e, key_l = kv_ref[0, :HALF, :HD], kv_ref[0, HALF:, :HD]
    val_e, val_l = kv_ref[0, :HALF, HD:], kv_ref[0, HALF:, HD:]
    key_p, val_p = prev_ref[0, :HALF, :HD], prev_ref[0, :HALF, HD:]
    key_o, val_o = prev_ref[0, pl.ds(offset, HALF), :HD], prev_ref[0, pl.ds(offset, HALF), HD:]
    lane = lax.broadcasted_iota(jnp.int32, (2 * HALF, HD), 1)
    deltas = jnp.zeros((2 * HALF, HD), F32)
    for h in range(heads):
        cols = slice(h * HD, (h + 1) * HD)
        row_sum = jnp.sum(
            do_ref[0, :, cols].astype(F32) * out_ref[0, :, cols].astype(F32), axis=1, keepdims=True
        )
        deltas = jnp.where(lane == h, row_sum, deltas)
    deltas = jnp.transpose(deltas)
    other_deltas = jnp.where(offset > 0, deltas[:, HALF:], deltas[:, :HALF])
    zero = jnp.zeros((HALF, HD), F32)
    dk_e, dk_l, dk_p, dk_o = zero, zero, zero, zero
    keys_late = jnp.concatenate([key_e, key_l, key_p], axis=0)
    for h in range(heads):
        cols = slice(h * HD, (h + 1) * HD)
        q_h, do_h = q_ref[0, :, cols], do_ref[0, :, cols]
        q_l, do_l = q_ref[0, HALF:, cols], do_ref[0, HALF:, cols]
        q_o, do_o = q_ref[0, pl.ds(offset, HALF), cols], do_ref[0, pl.ds(offset, HALF), cols]
        lse_e, lse_l = lse_ref[0, h : h + 1, :HALF], lse_ref[0, h : h + 1, HALF:]
        lse_o = lse_ref[0, h : h + 1, pl.ds(offset, HALF)]
        delta_e, delta_l = deltas[h : h + 1, :HALF], deltas[h : h + 1, HALF:]
        delta_o = other_deltas[h : h + 1]

        s_e, g_e = dot(key_e, q_h, NT), dot(val_e, do_h, NT)
        ds_ee = (prob_of(s_e[:, :HALF], lse_e, see_ee) * (g_e[:, :HALF] - delta_e)).astype(BF16)
        ds_el = (prob_of(s_e[:, HALF:], lse_l, see_el) * (g_e[:, HALF:] - delta_l)).astype(BF16)
        ds_ll = (
            prob_of(dot(key_l, q_l, NT), lse_l, see_ll) * (dot(val_l, do_l, NT) - delta_l)
        ).astype(BF16)
        ds_pl = (
            prob_of(dot(key_p, q_l, NT), lse_l, see_pl) * (dot(val_p, do_l, NT) - delta_l)
        ).astype(BF16)
        ds_o = (
            prob_of(dot(key_o, q_o, NT), lse_o, see_other) * (dot(val_o, do_o, NT) - delta_o)
        ).astype(BF16)
        dk_e = dk_e + dot(jnp.concatenate([ds_ee, ds_el], axis=1), q_h, NN)
        dk_l = dk_l + dot(ds_ll, q_l, NN)
        dk_p = dk_p + dot(ds_pl, q_l, NN)
        dk_o = dk_o + dot(ds_o, q_o, NN)
        acc_ref[:HALF] = dot(ds_ee, key_e, TN)
        acc_ref[HALF:] = dot(jnp.concatenate([ds_el, ds_ll, ds_pl], axis=0), keys_late, TN)
        acc_ref[pl.ds(offset, HALF)] += dot(ds_o, key_o, TN)
        dq_ref[0, :, cols] = (SCALING * acc_ref[...]).astype(BF16)
    is_first = offset > 0
    dk_ref[:HALF] = SCALING * dk_e
    dk_ref[HALF:] = SCALING * dk_l
    dk_prev_ref[:HALF] = (SCALING * jnp.where(is_first, dk_p, dk_p + dk_o)).astype(BF16)
    dk_prev_ref[HALF:] = (SCALING * jnp.where(is_first, dk_o, zero)).astype(BF16)


def call(body, outs, places, flops, moved, name, scratch=(), out_places=None):
    return pl.pallas_call(
        body,
        out_shape=outs,
        in_specs=[pl.BlockSpec(memory_space=place) for place in places],
        out_specs=[
            pl.BlockSpec(memory_space=place) for place in out_places or [pltpu.VMEM] * len(outs)
        ],
        scratch_shapes=list(scratch),
        compiler_params=pltpu.CompilerParams(vmem_limit_bytes=24 * 1024 * 1024),
        cost_estimate=pl.CostEstimate(flops=flops, bytes_accessed=moved, transcendentals=0),
        name=name,
    )


def sum_over(shares, rows):
    return jnp.sum(shares.reshape(-1, rows, HD).astype(F32), axis=0)


def scattered(partial, x_size, z_size):
    axes = ("context", "dp", "tensor")
    n_dp, n_tensor = lax.axis_size("dp"), lax.axis_size("tensor")

    def index(x, z, d, t):
        return ((x * z_size + z) * n_dp + d) * n_tensor + t

    first, second = [], []
    for t in range(n_tensor):
        odd = t % 2 == 1
        for fixed in range(x_size if not odd else z_size):
            for d in range(n_dp):
                first.append(
                    [index(j, fixed, d, t) for j in range(x_size)] if odd
                    else [index(fixed, j, d, t) for j in range(z_size)]
                )
        for fixed in range(z_size if not odd else x_size):
            second.append(
                [index(fixed, j, d, t) for j in range(z_size) for d in range(n_dp)] if odd
                else [index(j, fixed, d, t) for j in range(x_size) for d in range(n_dp)]
            )
    shares = lax.all_to_all(partial, axes, 0, 0, axis_index_groups=first, tiled=True)
    sums = sum_over(shares, partial.shape[0] // z_size).astype(BF16)
    shares = lax.all_to_all(sums, axes, 0, 0, axis_index_groups=second, tiled=True)
    return sum_over(shares, sums.shape[0] // (x_size * n_dp))


def per_device(queries, keys_values, outputs, grad_out, logsumexp, doc_ids, inputs):
    tok_rows = queries.shape[1]
    heads = queries.shape[2] // HD
    features = inputs.shape[2]
    cycle_size = lax.axis_size("context")
    x_size = z_size = math.isqrt(cycle_size)
    shape = jax.ShapeDtypeStruct
    hbm, vmem = pltpu.HBM, pltpu.VMEM

    queries, grad_out, logsumexp, doc_ids, inputs, outputs = (
        pltpu.with_memory_space_constraint(a, pltpu.HBM)
        for a in (queries, grad_out, logsumexp, doc_ids, inputs, outputs)
    )
    visiting = shifted(keys_values, "context", 1)
    dv_own, turned, q_near, kv_near, lse_near, do_near, docs_near = call(
        functools.partial(own_values, heads, cycle_size, x_size, z_size),
        [
            shape((tok_rows, HD), F32), shape((features, tok_rows), BF16),
            shape(queries.shape, BF16), shape(keys_values.shape, BF16),
            shape(logsumexp.shape, F32), shape(grad_out.shape, BF16),
            shape((2, 1, tok_rows), jnp.int32),
        ],
        [hbm] * 6, 400_000_000, 6_000_000, "own_values",
        scratch=[pltpu.VMEM(inputs.shape, BF16), pltpu.SemaphoreType.DMA((7,))],
    )(queries, keys_values, logsumexp, grad_out, doc_ids, inputs)
    (dv_prev,) = call(
        functools.partial(prev_values, heads), [shape((tok_rows, HD), BF16)],
        [vmem] * 5, 300_000_000, 1_200_000, "prev_values",
    )(q_near, visiting, lse_near, do_near, docs_near)
    dv_back = shifted(dv_prev, "context", -1)
    partial, dv_half = call(
        project, [shape((features, HD), BF16), shape((tok_rows, HD), BF16)],
        [vmem] * 3, 300_000_000, 3_000_000, "project",
        scratch=[pltpu.VMEM((features, HD), BF16), pltpu.SemaphoreType.DMA((8,))], out_places=[hbm, vmem],
    )(turned, dv_own, dv_back)
    proj_grad = scattered(partial, x_size, z_size)
    dq, dk_own, dk_prev = call(
        functools.partial(rest, heads),
        [
            shape(queries.shape, BF16), shape((tok_rows, HD), F32), shape((tok_rows, HD), BF16),
        ],
        [vmem] * 7 + [pl.ANY], 2_000_000_000, 3_000_000, "rest",
        scratch=[pltpu.VMEM((tok_rows, HD), F32)],
    )(q_near, kv_near, visiting, lse_near, do_near, outputs, docs_near, dv_half)
    dk_back = shifted(dk_prev, "context", -1)
    dk_half = (dk_own + dk_back.astype(F32)).astype(BF16)
    grad_kv = jnp.concatenate([dk_half, dv_half], axis=1)
    return dq, grad_kv[None], proj_grad[None]


def solution(mesh):
    in_specs = (
        P("dp", "context", "tensor"),
        P("dp", "context", "tensor"),
        P("dp", "context", "tensor"),
        P("dp", "context", "tensor"),
        P("dp", "tensor", "context"),
        P("dp", None),
        P("dp", "context", None),
    )
    out_specs = (
        P("dp", "context", "tensor"),
        P("dp", "context", "tensor"),
        P("tensor", ("context", "dp"), None),
    )
    return jax.shard_map(
        per_device, mesh=mesh, in_specs=in_specs, out_specs=out_specs, check_vma=False
    )
```

time: 93.3 us -> 81.8 us (0.88)
  the two profiles are of different devices: /device:TPU:2 before, /device:TPU:16 now
where the time goes in v2:
time: 81.8 us; the launch traced here: 81.4 us
  waiting for transfers between devices  35.4 us (43%)
  starting transfers between devices  31.3 us (38%)
  Pallas kernels  10.9 us (13%)
  other arithmetic  2.12 us (3%)
  local copies, waits for them, and re-layouts  0.91 us (1%)
    ppermute x3, starting transfers between devices, shifted(): return lax.ppermute(block, axis, route)  16.7 us
    ppermute x3, waiting for transfers between devices, shifted(): return lax.ppermute(block, axis, route)  16.7 us
    all_to_all x1, waiting for transfers between devices, scattered(): lax.all_to_all(sums, axes, 0, 0, axis_index_groups=second, tiled=True)  12.8 us
    all_to_all x1, starting transfers between devices, scattered(): lax.all_to_all(sums, axes, 0, 0, axis_index_groups=second, tiled=True)  11 us
    all_to_all x1, waiting for transfers between devices, scattered(): lax.all_to_all(partial, axes, 0, 0, axis_index_groups=first, tiled=True)  5.93 us
    pallas_call x1, Pallas kernels, per_device(): call(functools.partial(rest, heads), [shape(queries.shape, BF16), shape((...  5.06 us
    all_to_all x1, starting transfers between devices, scattered(): lax.all_to_all(partial, axes, 0, 0, axis_index_groups=first, tiled=True)  3.57 us
    pallas_call x1, Pallas kernels, per_device(): call(functools.partial(own_values, heads, cycle_size, x_size, z_size), [s...  3.02 us
  transfers between devices with their start and end apart: 5, of which 4 were waited for; matrix products, arithmetic and copies ran while one was open for 2% of the time, Pallas kernels for 10%

profile of v2, /device:TPU:16, one launch (start us, length us, event | category | flops | bytes accessed | tf_op | source)
XLA Modules:
  0.0 81.4 jit_solution(11546872241916801990)
XLA Ops:
  0.6 5.2 %collective-permute-start = (bf16[1,256,256]{2,1,0:T(8,128)(2,1)}, bf16[1,256,256]{2,1,0:T(8,128)(2,1)S(1)}, u32[]{:S(2)}, u32[]{:S(2)}) collective-permute-start(bf16[1,256,256]{2,1,0:T(8,128)(2,1)} %kv_hbm.1), channel_id=1, source_target_pairs={{1008,0},{0,16},{16,32},{32,48},{48,64},{64,80},{80,96},{96,112},{... | collective-permute-start | bytes 393224 | tf_op jit(solution)/shard_map/ppermute | solution.py:29
  5.8 0.0 copy-start
  5.8 0.9 %copy-done = bf16[1,256,256]{2,1,0:T(8,128)(2,1)S(1)} copy-done((bf16[1,256,256]{2,1,0:T(8,128)(2,1)S(1)}, bf16[1,256,256]{2,1,0:T(8,128)(2,1)}, u32[]{:S(2)}) %copy-start) | copy-done | bytes 131096
  6.7 3.0 %own_values.1 = (f32[256,128]{1,0:T(8,128)S(1)}, bf16[4096,256]{1,0:T(8,128)(2,1)S(1)}, bf16[1,256,1024]{2,1,0:T(8,128)(2,1)S(1)}, bf16[1,256,256]{2,1,0:T(8,128...) custom-call(bf16[1,256,1024]{2,1,0:T(8,128)(2,1)} %q_hbm.1, ...), custom_call_target="tpu_custom_call" | custom-call | flops 400000000 | bytes 6000000 | tf_op jit(solution)/shard_map/own_values/pallas_call | solution.py:286
  9.8 14.2 %collective-permute-done.kv_ref.prev_ref = bf16[1,256,256]{2,1,0:T(8,128)(2,1)S(1)} collective-permute-done((bf16[1,256,256]{2,1,0:T(8,128)(2,1)}, bf16[1,256,256]{2,1,0:T(8,128)(2,1)S(1)}, u32[]{:S(2)}, u32[]{:S(2)}) %collective-permute-start) | collective-permute-done | bytes 131104 | tf_op jit(solution)/shard_map/ppermute | solution.py:29
  24.0 1.3 %prev_values.1 = bf16[256,128]{1,0:T(8,128)(2,1)S(1)} custom-call(bf16[1,256,1024]{2,1,0:T(8,128)(2,1)S(1)} %get-tuple-element.15.q_ref, bf16[1,256,256]{2,1,0:T(8,128)(2,1)S(1)} %collective-permute-done.kv_ref.prev_ref, f32[1,8,256]{2,1,0:T(8,128)S(1)} %get-tuple-element.17.lse_ref, bf16[1,256,1024]{2,1,0:T(8,128)(2,1)S(1)} %get-tuple-element.18.do_ref, ...), custom_call_target="tpu_custom_call" | custom-call | flops 300000000 | bytes 1200000 | tf_op jit(solution)/shard_map/prev_values/pallas_call | solution.py:297
  25.3 3.6 %collective-permute-start.1 = (bf16[256,128]{1,0:T(8,128)(2,1)S(1)}, bf16[256,128]{1,0:T(8,128)(2,1)S(1)}, u32[]{:S(2)}, u32[]{:S(2)}) collective-permute-start(bf16[256,128]{1,0:T(8,128)(2,1)S(1)} %prev_values.1), channel_id=1, source_target_pairs={{16,0},{32,16},{48,32},{64,48},{80,64},{96,80},{112,96},{128,112},... | collective-permute-start | bytes 196616 | tf_op jit(solution)/shard_map/ppermute | solution.py:29
  28.9 2.5 %collective-permute-done.1.back_ref = bf16[256,128]{1,0:T(8,128)(2,1)S(1)} collective-permute-done((bf16[256,128]{1,0:T(8,128)(2,1)S(1)}, bf16[256,128]{1,0:T(8,128)(2,1)S(1)}, u32[]{:S(2)}, u32[]{:S(2)}) %collective-permute-start.1) | collective-permute-done | bytes 65568 | tf_op jit(solution)/shard_map/ppermute | solution.py:29
  31.4 1.5 %project.1 = (bf16[4096,128]{1,0:T(8,128)(2,1)}, bf16[256,128]{1,0:T(8,128)(2,1)S(1)}) custom-call(bf16[4096,256]{1,0:T(8,128)(2,1)S(1)} %get-tuple-element.20.xt_ref, f32[256,128]{1,0:T(8,128)S(1)} %get-tuple-element.21.own_ref, bf16[256,128]{1,0:T(8,128)(2,1)S(1)} %collective-permute-done.1.back_ref), custom_call_target="tpu_custom_call" | custom-call | flops 300000000 | bytes 3000000 | tf_op jit(solution)/shard_map/project/pallas_call | solution.py:302
  32.9 3.6 %all-to-all-start = ((bf16[8,512,128]{2,1,0:T(8,128)(2,1)}), bf16[8,512,128]{2,1,0:T(8,128)(2,1)S(1)}, u32[]{:S(2)}, u32[]{:S(2)}) async-start(bf16[8,512,128]{2,1,0:T(8,128)(2,1)} %bitcast.1), calls=%async_computation | async-start | bytes 2097152 | tf_op jit(solution)/shard_map/all_to_all | solution.py:266
  36.5 5.1 %rest.1 = (bf16[1,256,1024]{2,1,0:T(8,128)(2,1)}, f32[256,128]{1,0:T(8,128)S(1)}, bf16[256,128]{1,0:T(8,128)(2,1)S(1)}) custom-call(bf16[1,256,1024]{2,1,0:T(8,128)(2,1)S(1)} %get-tuple-element.15.q_ref, bf16[1,256,256]{2,1,0:T(8,128)(2,1)S(1)} %get-tuple-element.16.kv_ref, bf16[1,256,256]{2,1,0:T(8,128)(2,1)S(1)} %collective-permute-done.kv_ref.prev_ref, ...), custom_call_target="tpu_custom_call" | custom-call | flops 2000000000 | bytes 3000000 | tf_op jit(solution)/shard_map/rest/pallas_call | solution.py:308
  41.6 7.9 %collective-permute-start.2 = (bf16[256,128]{1,0:T(8,128)(2,1)S(1)}, bf16[256,128]{1,0:T(8,128)(2,1)S(1)}, u32[]{:S(2)}, u32[]{:S(2)}) collective-permute-start(bf16[256,128]{1,0:T(8,128)(2,1)S(1)} %get-tuple-element.25), channel_id=1, source_target_pairs={{16,0},{32,16},{48,32},{64,48},{80,64},{96,80},{112,96},{128,112},... | collective-permute-start | bytes 196616 | tf_op jit(solution)/shard_map/ppermute | solution.py:29
  49.5 5.9 %all-to-all-done = bf16[8,512,128]{2,1,0:T(8,128)(2,1)S(1)} async-done(((bf16[8,512,128]{2,1,0:T(8,128)(2,1)}), bf16[8,512,128]{2,1,0:T(8,128)(2,1)S(1)}, u32[]{:S(2)}, u32[]{:S(2)}) %all-to-all-start) | async-done | bytes 1048608 | tf_op jit(solution)/shard_map/all_to_all | solution.py:266
  55.4 0.8 reduce_sum.21
  56.2 11.0 %all-to-all-start.1 = ((bf16[16,32,128]{2,1,0:T(8,128)(2,1)}), bf16[16,32,128]{2,1,0:T(8,128)(2,1)S(1)}, u32[]{:S(2)}, u32[]{:S(2)}) async-start(bf16[16,32,128]{2,1,0:T(8,128)(2,1)} %bitcast.2), calls=%async_computation.1 | async-start | bytes 262144 | tf_op jit(solution)/shard_map/all_to_all | solution.py:268
  67.2 0.0 collective-permute-done.2
  67.3 0.7 maximum_bitcast_fusion
  67.9 12.8 %all-to-all-done.1 = bf16[16,32,128]{2,1,0:T(8,128)(2,1)S(1)} async-done(((bf16[16,32,128]{2,1,0:T(8,128)(2,1)}), bf16[16,32,128]{2,1,0:T(8,128)(2,1)S(1)}, u32[]{:S(2)}, u32[]{:S(2)}) %all-to-all-start.1) | async-done | bytes 131104 | tf_op jit(solution)/shard_map/all_to_all | solution.py:268
  80.7 0.6 convert_reduce_fusion
  (1 shorter events, 0.0 us)
Async XLA Ops:
  0.6 23.3 %collective-permute-start = (bf16[1,256,256]{2,1,0:T(8,128)(2,1)}, bf16[1,256,256]{2,1,0:T(8,128)(2,1)S(1)}, u32[]{:S(2)}, u32[]{:S(2)}) collective-permute-start(bf16[1,256,256]{2,1,0:T(8,128)(2,1)} %kv_hbm.1), channel_id=1, source_target_pairs={{1008,0},{0,16},{16,32},{32,48},{48,64},{64,80},{80,96},{96,112},{... | collective-permute-start | bytes 393224 | tf_op jit(solution)/shard_map/ppermute | solution.py:29
  5.8 0.9 %copy-start = (bf16[1,256,256]{2,1,0:T(8,128)(2,1)S(1)}, bf16[1,256,256]{2,1,0:T(8,128)(2,1)}, u32[]{:S(2)}) copy-start(bf16[1,256,256]{2,1,0:T(8,128)(2,1)} %kv_hbm.1) | copy-start | bytes 393220
  25.3 6.2 %collective-permute-start.1 = (bf16[256,128]{1,0:T(8,128)(2,1)S(1)}, bf16[256,128]{1,0:T(8,128)(2,1)S(1)}, u32[]{:S(2)}, u32[]{:S(2)}) collective-permute-start(bf16[256,128]{1,0:T(8,128)(2,1)S(1)} %prev_values.1), channel_id=1, source_target_pairs={{16,0},{32,16},{48,32},{64,48},{80,64},{96,80},{112,96},{128,112},... | collective-permute-start | bytes 196616 | tf_op jit(solution)/shard_map/ppermute | solution.py:29
  32.9 22.4 %all-to-all-start = ((bf16[8,512,128]{2,1,0:T(8,128)(2,1)}), bf16[8,512,128]{2,1,0:T(8,128)(2,1)S(1)}, u32[]{:S(2)}, u32[]{:S(2)}) async-start(bf16[8,512,128]{2,1,0:T(8,128)(2,1)} %bitcast.1), calls=%async_computation | async-start | bytes 2097152 | tf_op jit(solution)/shard_map/all_to_all | solution.py:266
  41.6 25.6 %collective-permute-start.2 = (bf16[256,128]{1,0:T(8,128)(2,1)S(1)}, bf16[256,128]{1,0:T(8,128)(2,1)S(1)}, u32[]{:S(2)}, u32[]{:S(2)}) collective-permute-start(bf16[256,128]{1,0:T(8,128)(2,1)S(1)} %get-tuple-element.25), channel_id=1, source_target_pairs={{16,0},{32,16},{48,32},{64,48},{80,64},{96,80},{112,96},{128,112},... | collective-permute-start | bytes 196616 | tf_op jit(solution)/shard_map/ppermute | solution.py:29
  56.2 24.5 %all-to-all-start.1 = ((bf16[16,32,128]{2,1,0:T(8,128)(2,1)}), bf16[16,32,128]{2,1,0:T(8,128)(2,1)S(1)}, u32[]{:S(2)}, u32[]{:S(2)}) async-start(bf16[16,32,128]{2,1,0:T(8,128)(2,1)} %bitcast.2), calls=%async_computation.1 | async-start | bytes 262144 | tf_op jit(solution)/shard_map/all_to_all | solution.py:268

commit v3 on v2

--- a/solution.py
+++ b/solution.py
@@ -66,7 +66,7 @@
 
 def swap_order(x_size, z_size):
     odd = lax.rem(lax.axis_index("tensor"), 2)
-    return lambda x, z: jnp.where(odd == 1, x * z_size + z, z * x_size + x)
+    return lambda x, z: jnp.where(odd == 0, x * z_size + z, z * x_size + x)
 
 
 def own_values(
@@ -162,6 +162,13 @@
         copy.wait()
 
 
+def add_up(shares_ref, sum_ref):
+    total = shares_ref[0].astype(F32)
+    for i in range(1, shares_ref.shape[0]):
+        total = total + shares_ref[i].astype(F32)
+    sum_ref[...] = total.astype(BF16)
+
+
 def rest(
     heads, q_ref, kv_ref, prev_ref, lse_ref, do_ref, out_ref, docs_ref, after_ref,
     dq_ref, dk_ref, dk_prev_ref, acc_ref,
@@ -251,20 +258,24 @@
 
     first, second = [], []
     for t in range(n_tensor):
-        odd = t % 2 == 1
-        for fixed in range(x_size if not odd else z_size):
+        x_first = t % 2 == 0
+        for fixed in range(x_size if not x_first else z_size):
             for d in range(n_dp):
                 first.append(
-                    [index(j, fixed, d, t) for j in range(x_size)] if odd
+                    [index(j, fixed, d, t) for j in range(x_size)] if x_first
                     else [index(fixed, j, d, t) for j in range(z_size)]
                 )
-        for fixed in range(z_size if not odd else x_size):
+        for fixed in range(z_size if not x_first else x_size):
             second.append(
-                [index(fixed, j, d, t) for j in range(z_size) for d in range(n_dp)] if odd
+                [index(fixed, j, d, t) for j in range(z_size) for d in range(n_dp)] if x_first
                 else [index(j, fixed, d, t) for j in range(x_size) for d in range(n_dp)]
             )
     shares = lax.all_to_all(partial, axes, 0, 0, axis_index_groups=first, tiled=True)
-    sums = sum_over(shares, partial.shape[0] // z_size).astype(BF16)
+    rows = partial.shape[0] // z_size
+    (sums,) = call(
+        add_up, [jax.ShapeDtypeStruct((rows, HD), BF16)], [pltpu.VMEM], 2_000_000, 1_200_000,
+        "add_up",
+    )(shares.reshape(z_size, rows, HD))
     shares = lax.all_to_all(sums, axes, 0, 0, axis_index_groups=second, tiled=True)
     return sum_over(shares, sums.shape[0] // (x_size * n_dp))
 
@@ -293,7 +304,10 @@
         ],
         [hbm] * 6, 400_000_000, 6_000_000, "own_values",
         scratch=[pltpu.VMEM(inputs.shape, BF16), pltpu.SemaphoreType.DMA((7,))],
-    )(queries, keys_values, logsumexp, grad_out, doc_ids, inputs)
+    )(
+        queries, pltpu.with_memory_space_constraint(keys_values, pltpu.HBM), logsumexp, grad_out,
+        doc_ids, inputs,
+    )
     (dv_prev,) = call(
         functools.partial(prev_values, heads), [shape((tok_rows, HD), BF16)],
         [vmem] * 5, 300_000_000, 1_200_000, "prev_values",

time: 81.8 us -> 81.2 us (level)
  local copies, waits for them, and re-layouts: 0.91 us -> 0 us
    all_to_all x1, starting transfers between devices: 11 us -> 10 us  [scattered(): lax.all_to_all(sums, axes, 0, 0, axis_index_groups=second, tiled=True)]
    unnamed x2 -> x0, local copies, waits for them, and re-layouts: 0.91 us -> none
    ppermute x3, waiting for transfers between devices: 16.7 us -> 17.6 us  [shifted(): return lax.ppermute(block, axis, route)]
    all_to_all x1, starting transfers between devices: 3.57 us -> 4.46 us  [scattered(): lax.all_to_all(partial, axes, 0, 0, axis_index_groups=first, tiled=True)]
  transfers between devices with their start and end apart: 5 -> 5, of which waited for: 4 -> 4; matrix products, arithmetic and copies ran while one was open for 2% -> 1% of each run, Pallas kernels for 10% -> 11%
where the time goes in v3:
time: 81.2 us; the launch traced here: 80.8 us
  waiting for transfers between devices  35.4 us (44%)
  starting transfers between devices  31.7 us (39%)
  Pallas kernels  11.7 us (14%)
  other arithmetic  1.32 us (2%)
    ppermute x3, waiting for transfers between devices, shifted(): return lax.ppermute(block, axis, route)  17.6 us
    ppermute x3, starting transfers between devices, shifted(): return lax.ppermute(block, axis, route)  17.2 us
    all_to_all x1, waiting for transfers between devices, scattered(): lax.all_to_all(sums, axes, 0, 0, axis_index_groups=second, tiled=True)  12.3 us
    all_to_all x1, starting transfers between devices, scattered(): lax.all_to_all(sums, axes, 0, 0, axis_index_groups=second, tiled=True)  10 us
    all_to_all x1, waiting for transfers between devices, scattered(): lax.all_to_all(partial, axes, 0, 0, axis_index_groups=first, tiled=True)  5.5 us
    pallas_call x1, Pallas kernels, per_device(): call(functools.partial(rest, heads), [shape(queries.shape, BF16), shape((...  5.05 us
    all_to_all x1, starting transfers between devices, scattered(): lax.all_to_all(partial, axes, 0, 0, axis_index_groups=first, tiled=True)  4.46 us
    pallas_call x1, Pallas kernels, per_device(): call(functools.partial(own_values, heads, cycle_size, x_size, z_size), [s...  3.03 us
  transfers between devices with their start and end apart: 5, of which 4 were waited for; matrix products, arithmetic and copies ran while one was open for 1% of the time, Pallas kernels for 11%

profile of v3, /device:TPU:16, one launch (start us, length us, event | category | flops | bytes accessed | tf_op | source)
XLA Modules:
  0.0 80.8 jit_solution(14704355977779695717)
XLA Ops:
  0.6 5.2 %collective-permute-start = (bf16[1,256,256]{2,1,0:T(8,128)(2,1)}, bf16[1,256,256]{2,1,0:T(8,128)(2,1)S(1)}, u32[]{:S(2)}, u32[]{:S(2)}) collective-permute-start(bf16[1,256,256]{2,1,0:T(8,128)(2,1)} %kv_hbm.1), channel_id=1, source_target_pairs={{1008,0},{0,16},{16,32},{32,48},{48,64},{64,80},{80,96},{96,112},{... | collective-permute-start | bytes 393224 | tf_op jit(solution)/shard_map/ppermute | solution.py:29
  5.8 3.0 %own_values.1 = (f32[256,128]{1,0:T(8,128)S(1)}, bf16[4096,256]{1,0:T(8,128)(2,1)S(1)}, bf16[1,256,1024]{2,1,0:T(8,128)(2,1)S(1)}, bf16[1,256,256]{2,1,0:T(8,128...) custom-call(bf16[1,256,1024]{2,1,0:T(8,128)(2,1)} %q_hbm.1, ...), custom_call_target="tpu_custom_call" | custom-call | flops 400000000 | bytes 6000000 | tf_op jit(solution)/shard_map/own_values/pallas_call | solution.py:297
  8.9 15.1 %collective-permute-done.kv_ref.prev_ref = bf16[1,256,256]{2,1,0:T(8,128)(2,1)S(1)} collective-permute-done((bf16[1,256,256]{2,1,0:T(8,128)(2,1)}, bf16[1,256,256]{2,1,0:T(8,128)(2,1)S(1)}, u32[]{:S(2)}, u32[]{:S(2)}) %collective-permute-start) | collective-permute-done | bytes 131104 | tf_op jit(solution)/shard_map/ppermute | solution.py:29
  24.0 1.3 %prev_values.1 = bf16[256,128]{1,0:T(8,128)(2,1)S(1)} custom-call(bf16[1,256,1024]{2,1,0:T(8,128)(2,1)S(1)} %get-tuple-element.15.q_ref, bf16[1,256,256]{2,1,0:T(8,128)(2,1)S(1)} %collective-permute-done.kv_ref.prev_ref, f32[1,8,256]{2,1,0:T(8,128)S(1)} %get-tuple-element.17.lse_ref, bf16[1,256,1024]{2,1,0:T(8,128)(2,1)S(1)} %get-tuple-element.18.do_ref, ...), custom_call_target="tpu_custom_call" | custom-call | flops 300000000 | bytes 1200000 | tf_op jit(solution)/shard_map/prev_values/pallas_call | solution.py:311
  25.3 3.6 %collective-permute-start.1 = (bf16[256,128]{1,0:T(8,128)(2,1)S(1)}, bf16[256,128]{1,0:T(8,128)(2,1)S(1)}, u32[]{:S(2)}, u32[]{:S(2)}) collective-permute-start(bf16[256,128]{1,0:T(8,128)(2,1)S(1)} %prev_values.1), channel_id=1, source_target_pairs={{16,0},{32,16},{48,32},{64,48},{80,64},{96,80},{112,96},{128,112},... | collective-permute-start | bytes 196616 | tf_op jit(solution)/shard_map/ppermute | solution.py:29
  28.9 2.5 %collective-permute-done.1.back_ref = bf16[256,128]{1,0:T(8,128)(2,1)S(1)} collective-permute-done((bf16[256,128]{1,0:T(8,128)(2,1)S(1)}, bf16[256,128]{1,0:T(8,128)(2,1)S(1)}, u32[]{:S(2)}, u32[]{:S(2)}) %collective-permute-start.1) | collective-permute-done | bytes 65568 | tf_op jit(solution)/shard_map/ppermute | solution.py:29
  31.4 1.5 %project.1 = (bf16[4096,128]{1,0:T(8,128)(2,1)}, bf16[256,128]{1,0:T(8,128)(2,1)S(1)}) custom-call(bf16[4096,256]{1,0:T(8,128)(2,1)S(1)} %get-tuple-element.20.xt_ref, f32[256,128]{1,0:T(8,128)S(1)} %get-tuple-element.21.own_ref, bf16[256,128]{1,0:T(8,128)(2,1)S(1)} %collective-permute-done.1.back_ref), custom_call_target="tpu_custom_call" | custom-call | flops 300000000 | bytes 3000000 | tf_op jit(solution)/shard_map/project/pallas_call | solution.py:316
  32.9 4.5 %all-to-all-start = ((bf16[8,512,128]{2,1,0:T(8,128)(2,1)}), bf16[8,512,128]{2,1,0:T(8,128)(2,1)S(1)}, u32[]{:S(2)}, u32[]{:S(2)}) async-start(bf16[8,512,128]{2,1,0:T(8,128)(2,1)} %bitcast.1), calls=%async_computation | async-start | bytes 2097152 | tf_op jit(solution)/shard_map/all_to_all | solution.py:273
  37.4 5.1 %rest.1 = (bf16[1,256,1024]{2,1,0:T(8,128)(2,1)}, f32[256,128]{1,0:T(8,128)S(1)}, bf16[256,128]{1,0:T(8,128)(2,1)S(1)}) custom-call(bf16[1,256,1024]{2,1,0:T(8,128)(2,1)S(1)} %get-tuple-element.15.q_ref, bf16[1,256,256]{2,1,0:T(8,128)(2,1)S(1)} %get-tuple-element.16.kv_ref, bf16[1,256,256]{2,1,0:T(8,128)(2,1)S(1)} %collective-permute-done.kv_ref.prev_ref, ...), custom_call_target="tpu_custom_call" | custom-call | flops 2000000000 | bytes 3000000 | tf_op jit(solution)/shard_map/rest/pallas_call | solution.py:322
  42.5 8.4 %collective-permute-start.2 = (bf16[256,128]{1,0:T(8,128)(2,1)S(1)}, bf16[256,128]{1,0:T(8,128)(2,1)S(1)}, u32[]{:S(2)}, u32[]{:S(2)}) collective-permute-start(bf16[256,128]{1,0:T(8,128)(2,1)S(1)} %get-tuple-element.25), channel_id=1, source_target_pairs={{16,0},{32,16},{48,32},{64,48},{80,64},{96,80},{112,96},{128,112},... | collective-permute-start | bytes 196616 | tf_op jit(solution)/shard_map/ppermute | solution.py:29
  50.9 5.5 %all-to-all-done.shares_ref = bf16[8,512,128]{2,1,0:T(8,128)(2,1)S(1)} async-done(((bf16[8,512,128]{2,1,0:T(8,128)(2,1)}), bf16[8,512,128]{2,1,0:T(8,128)(2,1)S(1)}, u32[]{:S(2)}, u32[]{:S(2)}) %all-to-all-start) | async-done | bytes 1048608 | tf_op jit(solution)/shard_map/all_to_all | solution.py:273
  56.4 0.8 add_up.1
  57.1 10.0 %all-to-all-start.1 = ((bf16[16,32,128]{2,1,0:T(8,128)(2,1)}), bf16[16,32,128]{2,1,0:T(8,128)(2,1)S(1)}, u32[]{:S(2)}, u32[]{:S(2)}) async-start(bf16[16,32,128]{2,1,0:T(8,128)(2,1)} %bitcast.2), calls=%async_computation.1 | async-start | bytes 262144 | tf_op jit(solution)/shard_map/all_to_all | solution.py:279
  67.2 0.0 collective-permute-done.2
  67.2 0.7 maximum_bitcast_fusion
  67.9 12.3 %all-to-all-done.1 = bf16[16,32,128]{2,1,0:T(8,128)(2,1)S(1)} async-done(((bf16[16,32,128]{2,1,0:T(8,128)(2,1)}), bf16[16,32,128]{2,1,0:T(8,128)(2,1)S(1)}, u32[]{:S(2)}, u32[]{:S(2)}) %all-to-all-start.1) | async-done | bytes 131104 | tf_op jit(solution)/shard_map/all_to_all | solution.py:279
  80.2 0.6 convert_reduce_fusion
  (1 shorter events, 0.0 us)
Async XLA Ops:
  0.6 23.3 %collective-permute-start = (bf16[1,256,256]{2,1,0:T(8,128)(2,1)}, bf16[1,256,256]{2,1,0:T(8,128)(2,1)S(1)}, u32[]{:S(2)}, u32[]{:S(2)}) collective-permute-start(bf16[1,256,256]{2,1,0:T(8,128)(2,1)} %kv_hbm.1), channel_id=1, source_target_pairs={{1008,0},{0,16},{16,32},{32,48},{48,64},{64,80},{80,96},{96,112},{... | collective-permute-start | bytes 393224 | tf_op jit(solution)/shard_map/ppermute | solution.py:29
  25.3 6.2 %collective-permute-start.1 = (bf16[256,128]{1,0:T(8,128)(2,1)S(1)}, bf16[256,128]{1,0:T(8,128)(2,1)S(1)}, u32[]{:S(2)}, u32[]{:S(2)}) collective-permute-start(bf16[256,128]{1,0:T(8,128)(2,1)S(1)} %prev_values.1), channel_id=1, source_target_pairs={{16,0},{32,16},{48,32},{64,48},{80,64},{96,80},{112,96},{128,112},... | collective-permute-start | bytes 196616 | tf_op jit(solution)/shard_map/ppermute | solution.py:29
  32.9 23.4 %all-to-all-start = ((bf16[8,512,128]{2,1,0:T(8,128)(2,1)}), bf16[8,512,128]{2,1,0:T(8,128)(2,1)S(1)}, u32[]{:S(2)}, u32[]{:S(2)}) async-start(bf16[8,512,128]{2,1,0:T(8,128)(2,1)} %bitcast.1), calls=%async_computation | async-start | bytes 2097152 | tf_op jit(solution)/shard_map/all_to_all | solution.py:273
  42.5 24.7 %collective-permute-start.2 = (bf16[256,128]{1,0:T(8,128)(2,1)S(1)}, bf16[256,128]{1,0:T(8,128)(2,1)S(1)}, u32[]{:S(2)}, u32[]{:S(2)}) collective-permute-start(bf16[256,128]{1,0:T(8,128)(2,1)S(1)} %get-tuple-element.25), channel_id=1, source_target_pairs={{16,0},{32,16},{48,32},{64,48},{80,64},{96,80},{112,96},{128,112},... | collective-permute-start | bytes 196616 | tf_op jit(solution)/shard_map/ppermute | solution.py:29
  57.1 23.0 %all-to-all-start.1 = ((bf16[16,32,128]{2,1,0:T(8,128)(2,1)}), bf16[16,32,128]{2,1,0:T(8,128)(2,1)S(1)}, u32[]{:S(2)}, u32[]{:S(2)}) async-start(bf16[16,32,128]{2,1,0:T(8,128)(2,1)} %bitcast.2), calls=%async_computation.1 | async-start | bytes 262144 | tf_op jit(solution)/shard_map/all_to_all | solution.py:279

commit v4 on v3

--- a/solution.py
+++ b/solution.py
@@ -125,24 +125,33 @@
 
 
 def prev_values(heads, q_ref, kv_ref, lse_ref, do_ref, docs_ref, dv_ref):
-    offset = other_offset()
-    see_late, see_other = prev_masks(docs_ref, offset > 0)
-    key_early, key_other = kv_ref[0, :HALF, :HD], kv_ref[0, pl.ds(offset, HALF), :HD]
-    first = jnp.zeros((HALF, HD), F32)
-    other = jnp.zeros((HALF, HD), F32)
-    for h in range(heads):
-        cols = slice(h * HD, (h + 1) * HD)
-        scores_late = dot(key_early, q_ref[0, HALF:, cols], NT)
-        scores_other = dot(key_other, q_ref[0, pl.ds(offset, HALF), cols], NT)
-        lse_l = lse_ref[0, h : h + 1, HALF:]
-        lse_o = lse_ref[0, h : h + 1, pl.ds(offset, HALF)]
-        prob_late = prob_of(scores_late, lse_l, see_late).astype(BF16)
-        prob_other = prob_of(scores_other, lse_o, see_other).astype(BF16)
-        first = first + dot(prob_late, do_ref[0, HALF:, cols], NN)
-        other = other + dot(prob_other, do_ref[0, pl.ds(offset, HALF), cols], NN)
-    is_first = offset > 0
-    dv_ref[:HALF] = jnp.where(is_first, first, first + other).astype(BF16)
-    dv_ref[HALF:] = jnp.where(is_first, other, jnp.zeros_like(other)).astype(BF16)
+    is_first = lax.axis_index("context") == 0
+    query_row = docs_ref[0].astype(F32)
+    key_early, key_late = halves(docs_ref, 1)
+    early_down = down(key_early)
+
+    @pl.when(jnp.logical_not(is_first))
+    def _():
+        visible = jnp.concatenate([early_down, early_down], axis=1) == query_row
+        total = jnp.zeros((HALF, HD), F32)
+        for h in range(heads):
+            cols = slice(h * HD, (h + 1) * HD)
+            scores = dot(kv_ref[0, :HALF, :HD], q_ref[0, :, cols], NT)
+            prob = prob_of(scores, lse_ref[0, h : h + 1, :], visible).astype(BF16)
+            total = total + dot(prob, do_ref[0, :, cols], NN)
+        dv_ref[:HALF] = total.astype(BF16)
+        dv_ref[HALF:] = jnp.zeros((HALF, HD), BF16)
+
+    @pl.when(is_first)
+    def _():
+        visible = jnp.concatenate([early_down, down(key_late)], axis=0) == query_row[:, HALF:]
+        total = jnp.zeros((2 * HALF, HD), F32)
+        for h in range(heads):
+            cols = slice(h * HD, (h + 1) * HD)
+            scores = dot(kv_ref[0, :, :HD], q_ref[0, HALF:, cols], NT)
+            prob = prob_of(scores, lse_ref[0, h : h + 1, HALF:], visible).astype(BF16)
+            total = total + dot(prob, do_ref[0, HALF:, cols], NN)
+        dv_ref[...] = total.astype(BF16)
 
 
 def project(xt_ref, own_ref, back_ref, part_hbm, dv_ref, part_ref, sems):

time: 81.2 us -> 80.6 us (level)
  no operation moved by 1% of the time
where the time goes in v4:
time: 80.6 us; the launch traced here: 80.3 us
  waiting for transfers between devices  35.3 us (44%)
  starting transfers between devices  31.9 us (40%)
  Pallas kernels  11 us (14%)
  other arithmetic  1.32 us (2%)
    ppermute x3, waiting for transfers between devices, shifted(): return lax.ppermute(block, axis, route)  17.5 us
    ppermute x3, starting transfers between devices, shifted(): return lax.ppermute(block, axis, route)  17.3 us
    all_to_all x1, waiting for transfers between devices, scattered(): lax.all_to_all(sums, axes, 0, 0, axis_index_groups=second, tiled=True)  12.3 us
    all_to_all x1, starting transfers between devices, scattered(): lax.all_to_all(sums, axes, 0, 0, axis_index_groups=second, tiled=True)  10 us
    all_to_all x1, waiting for transfers between devices, scattered(): lax.all_to_all(partial, axes, 0, 0, axis_index_groups=first, tiled=True)  5.5 us
    pallas_call x1, Pallas kernels, per_device(): call(functools.partial(rest, heads), [shape(queries.shape, BF16), shape((...  5.05 us
    all_to_all x1, starting transfers between devices, scattered(): lax.all_to_all(partial, axes, 0, 0, axis_index_groups=first, tiled=True)  4.56 us
    pallas_call x1, Pallas kernels, per_device(): call(functools.partial(own_values, heads, cycle_size, x_size, z_size), [s...  3.03 us
  transfers between devices with their start and end apart: 5, of which 4 were waited for; matrix products, arithmetic and copies ran while one was open for 1% of the time, Pallas kernels for 11%

profile of v4, /device:TPU:16, one launch (start us, length us, event | category | flops | bytes accessed | tf_op | source)
XLA Modules:
  0.0 80.3 jit_solution(9389146273626667156)
XLA Ops:
  0.6 5.2 %collective-permute-start = (bf16[1,256,256]{2,1,0:T(8,128)(2,1)}, bf16[1,256,256]{2,1,0:T(8,128)(2,1)S(1)}, u32[]{:S(2)}, u32[]{:S(2)}) collective-permute-start(bf16[1,256,256]{2,1,0:T(8,128)(2,1)} %kv_hbm.1), channel_id=1, source_target_pairs={{1008,0},{0,16},{16,32},{32,48},{48,64},{64,80},{80,96},{96,112},{... | collective-permute-start | bytes 393224 | tf_op jit(solution)/shard_map/ppermute | solution.py:29
  5.8 3.0 %own_values.1 = (f32[256,128]{1,0:T(8,128)S(1)}, bf16[4096,256]{1,0:T(8,128)(2,1)S(1)}, bf16[1,256,1024]{2,1,0:T(8,128)(2,1)S(1)}, bf16[1,256,256]{2,1,0:T(8,128...) custom-call(bf16[1,256,1024]{2,1,0:T(8,128)(2,1)} %q_hbm.1, ...), custom_call_target="tpu_custom_call" | custom-call | flops 400000000 | bytes 6000000 | tf_op jit(solution)/shard_map/own_values/pallas_call | solution.py:306
  8.9 15.1 %collective-permute-done.kv_ref.prev_ref = bf16[1,256,256]{2,1,0:T(8,128)(2,1)S(1)} collective-permute-done((bf16[1,256,256]{2,1,0:T(8,128)(2,1)}, bf16[1,256,256]{2,1,0:T(8,128)(2,1)S(1)}, u32[]{:S(2)}, u32[]{:S(2)}) %collective-permute-start) | collective-permute-done | bytes 131104 | tf_op jit(solution)/shard_map/ppermute | solution.py:29
  24.0 0.7 prev_values.1
  24.6 3.7 %collective-permute-start.1 = (bf16[256,128]{1,0:T(8,128)(2,1)S(1)}, bf16[256,128]{1,0:T(8,128)(2,1)S(1)}, u32[]{:S(2)}, u32[]{:S(2)}) collective-permute-start(bf16[256,128]{1,0:T(8,128)(2,1)S(1)} %prev_values.1), channel_id=1, source_target_pairs={{16,0},{32,16},{48,32},{64,48},{80,64},{96,80},{112,96},{128,112},... | collective-permute-start | bytes 196616 | tf_op jit(solution)/shard_map/ppermute | solution.py:29
  28.4 2.4 %collective-permute-done.1.back_ref = bf16[256,128]{1,0:T(8,128)(2,1)S(1)} collective-permute-done((bf16[256,128]{1,0:T(8,128)(2,1)S(1)}, bf16[256,128]{1,0:T(8,128)(2,1)S(1)}, u32[]{:S(2)}, u32[]{:S(2)}) %collective-permute-start.1) | collective-permute-done | bytes 65568 | tf_op jit(solution)/shard_map/ppermute | solution.py:29
  30.8 1.5 %project.1 = (bf16[4096,128]{1,0:T(8,128)(2,1)}, bf16[256,128]{1,0:T(8,128)(2,1)S(1)}) custom-call(bf16[4096,256]{1,0:T(8,128)(2,1)S(1)} %get-tuple-element.20.xt_ref, f32[256,128]{1,0:T(8,128)S(1)} %get-tuple-element.21.own_ref, bf16[256,128]{1,0:T(8,128)(2,1)S(1)} %collective-permute-done.1.back_ref), custom_call_target="tpu_custom_call" | custom-call | flops 300000000 | bytes 3000000 | tf_op jit(solution)/shard_map/project/pallas_call | solution.py:325
  32.3 4.6 %all-to-all-start = ((bf16[8,512,128]{2,1,0:T(8,128)(2,1)}), bf16[8,512,128]{2,1,0:T(8,128)(2,1)S(1)}, u32[]{:S(2)}, u32[]{:S(2)}) async-start(bf16[8,512,128]{2,1,0:T(8,128)(2,1)} %bitcast.1), calls=%async_computation | async-start | bytes 2097152 | tf_op jit(solution)/shard_map/all_to_all | solution.py:282
  36.9 5.1 %rest.1 = (bf16[1,256,1024]{2,1,0:T(8,128)(2,1)}, f32[256,128]{1,0:T(8,128)S(1)}, bf16[256,128]{1,0:T(8,128)(2,1)S(1)}) custom-call(bf16[1,256,1024]{2,1,0:T(8,128)(2,1)S(1)} %get-tuple-element.15.q_ref, bf16[1,256,256]{2,1,0:T(8,128)(2,1)S(1)} %get-tuple-element.16.kv_ref, bf16[1,256,256]{2,1,0:T(8,128)(2,1)S(1)} %collective-permute-done.kv_ref.prev_ref, ...), custom_call_target="tpu_custom_call" | custom-call | flops 2000000000 | bytes 3000000 | tf_op jit(solution)/shard_map/rest/pallas_call | solution.py:331
  41.9 8.4 %collective-permute-start.2 = (bf16[256,128]{1,0:T(8,128)(2,1)S(1)}, bf16[256,128]{1,0:T(8,128)(2,1)S(1)}, u32[]{:S(2)}, u32[]{:S(2)}) collective-permute-start(bf16[256,128]{1,0:T(8,128)(2,1)S(1)} %get-tuple-element.25), channel_id=1, source_target_pairs={{16,0},{32,16},{48,32},{64,48},{80,64},{96,80},{112,96},{128,112},... | collective-permute-start | bytes 196616 | tf_op jit(solution)/shard_map/ppermute | solution.py:29
  50.3 5.5 %all-to-all-done.shares_ref = bf16[8,512,128]{2,1,0:T(8,128)(2,1)S(1)} async-done(((bf16[8,512,128]{2,1,0:T(8,128)(2,1)}), bf16[8,512,128]{2,1,0:T(8,128)(2,1)S(1)}, u32[]{:S(2)}, u32[]{:S(2)}) %all-to-all-start) | async-done | bytes 1048608 | tf_op jit(solution)/shard_map/all_to_all | solution.py:282
  55.8 0.8 add_up.1
  56.6 10.0 %all-to-all-start.1 = ((bf16[16,32,128]{2,1,0:T(8,128)(2,1)}), bf16[16,32,128]{2,1,0:T(8,128)(2,1)S(1)}, u32[]{:S(2)}, u32[]{:S(2)}) async-start(bf16[16,32,128]{2,1,0:T(8,128)(2,1)} %bitcast.2), calls=%async_computation.1 | async-start | bytes 262144 | tf_op jit(solution)/shard_map/all_to_all | solution.py:288
  66.6 0.0 collective-permute-done.2
  66.7 0.7 maximum_bitcast_fusion
  67.4 12.3 %all-to-all-done.1 = bf16[16,32,128]{2,1,0:T(8,128)(2,1)S(1)} async-done(((bf16[16,32,128]{2,1,0:T(8,128)(2,1)}), bf16[16,32,128]{2,1,0:T(8,128)(2,1)S(1)}, u32[]{:S(2)}, u32[]{:S(2)}) %all-to-all-start.1) | async-done | bytes 131104 | tf_op jit(solution)/shard_map/all_to_all | solution.py:288
  79.6 0.6 convert_reduce_fusion
  (1 shorter events, 0.0 us)
Async XLA Ops:
  0.6 23.3 %collective-permute-start = (bf16[1,256,256]{2,1,0:T(8,128)(2,1)}, bf16[1,256,256]{2,1,0:T(8,128)(2,1)S(1)}, u32[]{:S(2)}, u32[]{:S(2)}) collective-permute-start(bf16[1,256,256]{2,1,0:T(8,128)(2,1)} %kv_hbm.1), channel_id=1, source_target_pairs={{1008,0},{0,16},{16,32},{32,48},{48,64},{64,80},{80,96},{96,112},{... | collective-permute-start | bytes 393224 | tf_op jit(solution)/shard_map/ppermute | solution.py:29
  24.6 6.2 %collective-permute-start.1 = (bf16[256,128]{1,0:T(8,128)(2,1)S(1)}, bf16[256,128]{1,0:T(8,128)(2,1)S(1)}, u32[]{:S(2)}, u32[]{:S(2)}) collective-permute-start(bf16[256,128]{1,0:T(8,128)(2,1)S(1)} %prev_values.1), channel_id=1, source_target_pairs={{16,0},{32,16},{48,32},{64,48},{80,64},{96,80},{112,96},{128,112},... | collective-permute-start | bytes 196616 | tf_op jit(solution)/shard_map/ppermute | solution.py:29
  32.3 23.5 %all-to-all-start = ((bf16[8,512,128]{2,1,0:T(8,128)(2,1)}), bf16[8,512,128]{2,1,0:T(8,128)(2,1)S(1)}, u32[]{:S(2)}, u32[]{:S(2)}) async-start(bf16[8,512,128]{2,1,0:T(8,128)(2,1)} %bitcast.1), calls=%async_computation | async-start | bytes 2097152 | tf_op jit(solution)/shard_map/all_to_all | solution.py:282
  41.9 24.7 %collective-permute-start.2 = (bf16[256,128]{1,0:T(8,128)(2,1)S(1)}, bf16[256,128]{1,0:T(8,128)(2,1)S(1)}, u32[]{:S(2)}, u32[]{:S(2)}) collective-permute-start(bf16[256,128]{1,0:T(8,128)(2,1)S(1)} %get-tuple-element.25), channel_id=1, source_target_pairs={{16,0},{32,16},{48,32},{64,48},{80,64},{96,80},{112,96},{128,112},... | collective-permute-start | bytes 196616 | tf_op jit(solution)/shard_map/ppermute | solution.py:29
  56.6 23.0 %all-to-all-start.1 = ((bf16[16,32,128]{2,1,0:T(8,128)(2,1)}), bf16[16,32,128]{2,1,0:T(8,128)(2,1)S(1)}, u32[]{:S(2)}, u32[]{:S(2)}) async-start(bf16[16,32,128]{2,1,0:T(8,128)(2,1)} %bitcast.2), calls=%async_computation.1 | async-start | bytes 262144 | tf_op jit(solution)/shard_map/all_to_all | solution.py:288

commit v5 on v4

--- a/solution.py
+++ b/solution.py
@@ -325,7 +325,7 @@
     partial, dv_half = call(
         project, [shape((features, HD), BF16), shape((tok_rows, HD), BF16)],
         [vmem] * 3, 300_000_000, 3_000_000, "project",
-        scratch=[pltpu.VMEM((features, HD), BF16), pltpu.SemaphoreType.DMA((8,))], out_places=[hbm, vmem],
+        scratch=[pltpu.VMEM((features, HD), BF16), pltpu.SemaphoreType.DMA((16,))], out_places=[hbm, vmem],
     )(turned, dv_own, dv_back)
     proj_grad = scattered(partial, x_size, z_size)
     dq, dk_own, dk_prev = call(

time: 80.6 us -> 80.6 us (level)
  no operation moved by 1% of the time
where the time goes in v5:
time: 80.6 us; the launch traced here: 80.3 us
  waiting for transfers between devices  35.3 us (44%)
  starting transfers between devices  31.9 us (40%)
  Pallas kernels  11 us (14%)
  other arithmetic  1.32 us (2%)
    ppermute x3, waiting for transfers between devices, shifted(): return lax.ppermute(block, axis, route)  17.5 us
    ppermute x3, starting transfers between devices, shifted(): return lax.ppermute(block, axis, route)  17.3 us
    all_to_all x1, waiting for transfers between devices, scattered(): lax.all_to_all(sums, axes, 0, 0, axis_index_groups=second, tiled=True)  12.3 us
    all_to_all x1, starting transfers between devices, scattered(): lax.all_to_all(sums, axes, 0, 0, axis_index_groups=second, tiled=True)  10 us
    all_to_all x1, waiting for transfers between devices, scattered(): lax.all_to_all(partial, axes, 0, 0, axis_index_groups=first, tiled=True)  5.51 us
    pallas_call x1, Pallas kernels, per_device(): call(functools.partial(rest, heads), [shape(queries.shape, BF16), shape((...  5.06 us
    all_to_all x1, starting transfers between devices, scattered(): lax.all_to_all(partial, axes, 0, 0, axis_index_groups=first, tiled=True)  4.56 us
    pallas_call x1, Pallas kernels, per_device(): call(functools.partial(own_values, heads, cycle_size, x_size, z_size), [s...  3.03 us
  transfers between devices with their start and end apart: 5, of which 4 were waited for; matrix products, arithmetic and copies ran while one was open for 1% of the time, Pallas kernels for 11%

profile of v5, /device:TPU:16, one launch (start us, length us, event | category | flops | bytes accessed | tf_op | source)
XLA Modules:
  0.0 80.3 jit_solution(6860942450729348104)
XLA Ops:
  0.6 5.2 %collective-permute-start = (bf16[1,256,256]{2,1,0:T(8,128)(2,1)}, bf16[1,256,256]{2,1,0:T(8,128)(2,1)S(1)}, u32[]{:S(2)}, u32[]{:S(2)}) collective-permute-start(bf16[1,256,256]{2,1,0:T(8,128)(2,1)} %kv_hbm.1), channel_id=1, source_target_pairs={{1008,0},{0,16},{16,32},{32,48},{48,64},{64,80},{80,96},{96,112},{... | collective-permute-start | bytes 393224 | tf_op jit(solution)/shard_map/ppermute | solution.py:29
  5.8 3.0 %own_values.1 = (f32[256,128]{1,0:T(8,128)S(1)}, bf16[4096,256]{1,0:T(8,128)(2,1)S(1)}, bf16[1,256,1024]{2,1,0:T(8,128)(2,1)S(1)}, bf16[1,256,256]{2,1,0:T(8,128...) custom-call(bf16[1,256,1024]{2,1,0:T(8,128)(2,1)} %q_hbm.1, ...), custom_call_target="tpu_custom_call" | custom-call | flops 400000000 | bytes 6000000 | tf_op jit(solution)/shard_map/own_values/pallas_call | solution.py:306
  8.9 15.1 %collective-permute-done.kv_ref.prev_ref = bf16[1,256,256]{2,1,0:T(8,128)(2,1)S(1)} collective-permute-done((bf16[1,256,256]{2,1,0:T(8,128)(2,1)}, bf16[1,256,256]{2,1,0:T(8,128)(2,1)S(1)}, u32[]{:S(2)}, u32[]{:S(2)}) %collective-permute-start) | collective-permute-done | bytes 131104 | tf_op jit(solution)/shard_map/ppermute | solution.py:29
  24.0 0.7 prev_values.1
  24.6 3.7 %collective-permute-start.1 = (bf16[256,128]{1,0:T(8,128)(2,1)S(1)}, bf16[256,128]{1,0:T(8,128)(2,1)S(1)}, u32[]{:S(2)}, u32[]{:S(2)}) collective-permute-start(bf16[256,128]{1,0:T(8,128)(2,1)S(1)} %prev_values.1), channel_id=1, source_target_pairs={{16,0},{32,16},{48,32},{64,48},{80,64},{96,80},{112,96},{128,112},... | collective-permute-start | bytes 196616 | tf_op jit(solution)/shard_map/ppermute | solution.py:29
  28.4 2.4 %collective-permute-done.1.back_ref = bf16[256,128]{1,0:T(8,128)(2,1)S(1)} collective-permute-done((bf16[256,128]{1,0:T(8,128)(2,1)S(1)}, bf16[256,128]{1,0:T(8,128)(2,1)S(1)}, u32[]{:S(2)}, u32[]{:S(2)}) %collective-permute-start.1) | collective-permute-done | bytes 65568 | tf_op jit(solution)/shard_map/ppermute | solution.py:29
  30.8 1.5 %project.1 = (bf16[4096,128]{1,0:T(8,128)(2,1)}, bf16[256,128]{1,0:T(8,128)(2,1)S(1)}) custom-call(bf16[4096,256]{1,0:T(8,128)(2,1)S(1)} %get-tuple-element.20.xt_ref, f32[256,128]{1,0:T(8,128)S(1)} %get-tuple-element.21.own_ref, bf16[256,128]{1,0:T(8,128)(2,1)S(1)} %collective-permute-done.1.back_ref), custom_call_target="tpu_custom_call" | custom-call | flops 300000000 | bytes 3000000 | tf_op jit(solution)/shard_map/project/pallas_call | solution.py:325
  32.3 4.6 %all-to-all-start = ((bf16[8,512,128]{2,1,0:T(8,128)(2,1)}), bf16[8,512,128]{2,1,0:T(8,128)(2,1)S(1)}, u32[]{:S(2)}, u32[]{:S(2)}) async-start(bf16[8,512,128]{2,1,0:T(8,128)(2,1)} %bitcast.1), calls=%async_computation | async-start | bytes 2097152 | tf_op jit(solution)/shard_map/all_to_all | solution.py:282
  36.9 5.1 %rest.1 = (bf16[1,256,1024]{2,1,0:T(8,128)(2,1)}, f32[256,128]{1,0:T(8,128)S(1)}, bf16[256,128]{1,0:T(8,128)(2,1)S(1)}) custom-call(bf16[1,256,1024]{2,1,0:T(8,128)(2,1)S(1)} %get-tuple-element.15.q_ref, bf16[1,256,256]{2,1,0:T(8,128)(2,1)S(1)} %get-tuple-element.16.kv_ref, bf16[1,256,256]{2,1,0:T(8,128)(2,1)S(1)} %collective-permute-done.kv_ref.prev_ref, ...), custom_call_target="tpu_custom_call" | custom-call | flops 2000000000 | bytes 3000000 | tf_op jit(solution)/shard_map/rest/pallas_call | solution.py:331
  41.9 8.4 %collective-permute-start.2 = (bf16[256,128]{1,0:T(8,128)(2,1)S(1)}, bf16[256,128]{1,0:T(8,128)(2,1)S(1)}, u32[]{:S(2)}, u32[]{:S(2)}) collective-permute-start(bf16[256,128]{1,0:T(8,128)(2,1)S(1)} %get-tuple-element.25), channel_id=1, source_target_pairs={{16,0},{32,16},{48,32},{64,48},{80,64},{96,80},{112,96},{128,112},... | collective-permute-start | bytes 196616 | tf_op jit(solution)/shard_map/ppermute | solution.py:29
  50.3 5.5 %all-to-all-done.shares_ref = bf16[8,512,128]{2,1,0:T(8,128)(2,1)S(1)} async-done(((bf16[8,512,128]{2,1,0:T(8,128)(2,1)}), bf16[8,512,128]{2,1,0:T(8,128)(2,1)S(1)}, u32[]{:S(2)}, u32[]{:S(2)}) %all-to-all-start) | async-done | bytes 1048608 | tf_op jit(solution)/shard_map/all_to_all | solution.py:282
  55.8 0.8 add_up.1
  56.6 10.0 %all-to-all-start.1 = ((bf16[16,32,128]{2,1,0:T(8,128)(2,1)}), bf16[16,32,128]{2,1,0:T(8,128)(2,1)S(1)}, u32[]{:S(2)}, u32[]{:S(2)}) async-start(bf16[16,32,128]{2,1,0:T(8,128)(2,1)} %bitcast.2), calls=%async_computation.1 | async-start | bytes 262144 | tf_op jit(solution)/shard_map/all_to_all | solution.py:288
  66.7 0.0 collective-permute-done.2
  66.7 0.7 maximum_bitcast_fusion
  67.4 12.3 %all-to-all-done.1 = bf16[16,32,128]{2,1,0:T(8,128)(2,1)S(1)} async-done(((bf16[16,32,128]{2,1,0:T(8,128)(2,1)}), bf16[16,32,128]{2,1,0:T(8,128)(2,1)S(1)}, u32[]{:S(2)}, u32[]{:S(2)}) %all-to-all-start.1) | async-done | bytes 131104 | tf_op jit(solution)/shard_map/all_to_all | solution.py:288
  79.6 0.6 convert_reduce_fusion
  (1 shorter events, 0.0 us)
Async XLA Ops:
  0.6 23.3 %collective-permute-start = (bf16[1,256,256]{2,1,0:T(8,128)(2,1)}, bf16[1,256,256]{2,1,0:T(8,128)(2,1)S(1)}, u32[]{:S(2)}, u32[]{:S(2)}) collective-permute-start(bf16[1,256,256]{2,1,0:T(8,128)(2,1)} %kv_hbm.1), channel_id=1, source_target_pairs={{1008,0},{0,16},{16,32},{32,48},{48,64},{64,80},{80,96},{96,112},{... | collective-permute-start | bytes 393224 | tf_op jit(solution)/shard_map/ppermute | solution.py:29
  24.6 6.2 %collective-permute-start.1 = (bf16[256,128]{1,0:T(8,128)(2,1)S(1)}, bf16[256,128]{1,0:T(8,128)(2,1)S(1)}, u32[]{:S(2)}, u32[]{:S(2)}) collective-permute-start(bf16[256,128]{1,0:T(8,128)(2,1)S(1)} %prev_values.1), channel_id=1, source_target_pairs={{16,0},{32,16},{48,32},{64,48},{80,64},{96,80},{112,96},{128,112},... | collective-permute-start | bytes 196616 | tf_op jit(solution)/shard_map/ppermute | solution.py:29
  32.3 23.5 %all-to-all-start = ((bf16[8,512,128]{2,1,0:T(8,128)(2,1)}), bf16[8,512,128]{2,1,0:T(8,128)(2,1)S(1)}, u32[]{:S(2)}, u32[]{:S(2)}) async-start(bf16[8,512,128]{2,1,0:T(8,128)(2,1)} %bitcast.1), calls=%async_computation | async-start | bytes 2097152 | tf_op jit(solution)/shard_map/all_to_all | solution.py:282
  41.9 24.7 %collective-permute-start.2 = (bf16[256,128]{1,0:T(8,128)(2,1)S(1)}, bf16[256,128]{1,0:T(8,128)(2,1)S(1)}, u32[]{:S(2)}, u32[]{:S(2)}) collective-permute-start(bf16[256,128]{1,0:T(8,128)(2,1)S(1)} %get-tuple-element.25), channel_id=1, source_target_pairs={{16,0},{32,16},{48,32},{64,48},{80,64},{96,80},{112,96},{128,112},... | collective-permute-start | bytes 196616 | tf_op jit(solution)/shard_map/ppermute | solution.py:29
  56.6 23.0 %all-to-all-start.1 = ((bf16[16,32,128]{2,1,0:T(8,128)(2,1)}), bf16[16,32,128]{2,1,0:T(8,128)(2,1)S(1)}, u32[]{:S(2)}, u32[]{:S(2)}) async-start(bf16[16,32,128]{2,1,0:T(8,128)(2,1)} %bitcast.2), calls=%async_computation.1 | async-start | bytes 262144 | tf_op jit(solution)/shard_map/all_to_all | solution.py:288
